TPU v7x, 32 devices: a whole 2x2x4 slice. The times are simulated.
32 devices in a mesh: dp: 16 (over z, y, core), branch: 2 (over x).
Axes of the slice: x: 2, y: 2, z: 4, core: 2. Of those that a mesh axis runs over, the one named last changes fastest.
Arguments:
- stream: bfloat16 [16384, 1024], P(('dp', 'branch')), may hold values from -6 to 6
- cotangent: bfloat16 [16384, 1024], P(('dp', 'branch')), may hold values from -6 to 6
- lengths: int32 [16], P('dp'), may hold values from 128 to 1024, as said below
- steps_taken: int32 [1], replicated, may hold values from 2 to 20
- learning_rates: float32 [6], replicated
- mixing: float32 [1024, 3072], P(('dp', 'branch')), may hold values from -0.1875 to 0.1875
- merging: float32 [1024, 1024], P(('dp', 'branch')), may hold values from -3 to 3
- expand: float32 [1024, 4096], P(('dp', 'branch')), may hold values from -0.1875 to 0.1875
- shrink: float32 [4096, 1024], P(('dp', 'branch')), may hold values from -0.09375 to 0.09375
- vectors: float32 [2, 1024], P(None, ('dp', 'branch')), may hold values from -1 to 2
- offsets: float32 [5120], P(('dp', 'branch')), may hold values from -1.75 to 1.75
- mixing_momentum: float32 [1024, 3072], P(('dp', 'branch'))
- merging_momentum: float32 [1024, 1024], P(('dp', 'branch'))
- expand_momentum: float32 [1024, 4096], P(('dp', 'branch'))
- shrink_momentum: float32 [4096, 1024], P(('dp', 'branch'))
- vectors_momentum: float32 [2, 1024], P(None, ('dp', 'branch'))
- offsets_momentum: float32 [5120], P(('dp', 'branch'))
- mixing_variance: float32 [1024, 3072], P(('dp', 'branch'))
- merging_variance: float32 [1024, 1024], P(('dp', 'branch'))
- expand_variance: float32 [1024, 4096], P(('dp', 'branch'))
- shrink_variance: float32 [4096, 1024], P(('dp', 'branch'))
- vectors_variance: float32 [2, 1024], P(None, ('dp', 'branch'))
- offsets_variance: float32 [5120], P(('dp', 'branch'))
Outputs:
- residual: bfloat16 [16384, 1024], P(('dp', 'branch'))
- stream_grad: float32 [16384, 1024], P(('dp', 'branch'))
- mixing_next: float32 [1024, 3072], P(('dp', 'branch'))
- mixing_half: bfloat16 [1024, 3072], P(('dp', 'branch'))
- mixing_drift: float32 [1024, 3072], P(('dp', 'branch'))
- mixing_power: float32 [1024, 3072], P(('dp', 'branch'))
- merging_next: float32 [1024, 1024], P(('dp', 'branch'))
- merging_half: bfloat16 [1024, 1024], P(('dp', 'branch'))
- merging_drift: float32 [1024, 1024], P(('dp', 'branch'))
- merging_power: float32 [1024, 1024], P(('dp', 'branch'))
- expand_next: float32 [1024, 4096], P(('dp', 'branch'))
- expand_half: bfloat16 [1024, 4096], P(('dp', 'branch'))
- expand_drift: float32 [1024, 4096], P(('dp', 'branch'))
- expand_power: float32 [1024, 4096], P(('dp', 'branch'))
- shrink_next: float32 [4096, 1024], P(('dp', 'branch'))
- shrink_half: bfloat16 [4096, 1024], P(('dp', 'branch'))
- shrink_drift: float32 [4096, 1024], P(('dp', 'branch'))
- shrink_power: float32 [4096, 1024], P(('dp', 'branch'))
- vectors_next: float32 [2, 1024], P(None, ('dp', 'branch'))
- vectors_half: bfloat16 [2, 1024], P(None, ('dp', 'branch'))
- vectors_drift: float32 [2, 1024], P(None, ('dp', 'branch'))
- vectors_power: float32 [2, 1024], P(None, ('dp', 'branch'))
- offsets_next: float32 [5120], P(('dp', 'branch'))
- offsets_half: bfloat16 [5120], P(('dp', 'branch'))
- offsets_drift: float32 [5120], P(('dp', 'branch'))
- offsets_power: float32 [5120], P(('dp', 'branch'))
Inputs may be any that keep to these rules, and one draw needn't show every extreme that they name: `lengths`: at least one protein of all has exactly 1024 residues.
All inputs are finite; a program needn't handle non-finite values.
Results may differ from a plain program's by a relative error of at most 0.01.
The roundings to bfloat16 on the way count: a program that leaves them out, or rounds other values in their place, can miss the bound.
Values may be sent and summed in bfloat16 or wider, within the bound.
A program may use at most 256 MiB of HBM per device.

v0:
```python
import functools

import jax
import jax.numpy as jnp
import numpy as np
from jax import lax
from jax.experimental import pallas as pl
from jax.experimental.pallas import tpu as pltpu
from jax.sharding import PartitionSpec as P

HEAD = 64
ROT = 32
beta_one = 0.9
beta_two = 0.95
adam_eps = 1e-08
decay_rate = 0.1
norm_eps = 1e-05
rope_base = 10000.0
masked_score = -1e30
BF = jnp.bfloat16
F32 = jnp.float32


def dot(left, right):
    return jnp.dot(left, right, preferred_element_type=F32)


def dot_left(left, right):
    return lax.dot_general(left, right, (((0,), (0,)), ((), ())), preferred_element_type=F32)


def dot_right(left, right):
    return lax.dot_general(left, right, (((1,), (1,)), ((), ())), preferred_element_type=F32)


def rope_tables(length):
    places = np.arange(length, dtype=np.float32)[:, None]
    column = np.arange(2 * HEAD) % HEAD
    paired = (column // 2).astype(np.float32)
    frequency = np.exp(paired * np.float32(-2.0 / ROT) * np.log(np.float32(rope_base)))
    angles = (places * frequency[None, :].astype(np.float32)).astype(np.float64)
    inside = (column < ROT)[None, :]
    signed = np.where(column % 2 == 0, -1.0, 1.0)[None, :]
    cosine = np.where(inside, np.cos(angles), 1.0).astype(np.float32)
    sine = np.where(inside, np.sin(angles) * signed, 0.0).astype(np.float32)
    return cosine, sine


def adam_update(master, gradient, momentum, variance, rate, count, decay):
    drift = beta_one * momentum + (1.0 - beta_one) * gradient
    power = beta_two * variance + (1.0 - beta_two) * gradient * gradient
    first_fix = 1.0 - jnp.power(beta_one, count)
    second_fix = 1.0 - jnp.power(beta_two, count)
    moved = drift / first_fix / (jnp.sqrt(power / second_fix) + adam_eps)
    updated = master - rate * (moved + decay * master)
    return (updated, updated.astype(BF), drift, power)


class Plan:
    def __init__(self, n, stream, mixing, merging, expand, shrink, vectors, offsets):
        self.n = n
        self.own_rows, self.D = stream.shape
        self.rows = 2 * self.own_rows
        self.W = self.D // 2
        self.FF = expand.shape[1]
        self.rq = mixing.shape[0]
        self.rr = merging.shape[0]
        self.mr = max(16, self.rr)
        self.hb = shrink.shape[0]
        self.C = 4 if self.hb >= 64 else 2
        self.q = self.hb // self.C
        self.CW = self.FF // 2 // self.C
        self.wb = self.D // self.CW
        self.vc = vectors.shape[1]
        self.ow = offsets.shape[0]
        self.o_merge = 6 * self.rq
        self.o_small = self.o_merge + 2 * self.mr
        self.g_rows = self.o_small + 16
        self.c_rows = 2 * self.rq + self.wb * self.q


MESH = pl.DeviceIdType.MESH
BLOCK = 256
ATTEND_SHARE = 14
LATE = 2
AB_START = 1.0
AB_STEP = 6.0
C_START = 0.5
C_STEP = 5.0


def turned(a, cosine, sine, back):
    lanes = a.shape[1]
    even = lax.broadcasted_iota(jnp.int32, a.shape, 1) % 2 == 0
    t = a * sine if back else a
    swapped = jnp.where(even, pltpu.roll(t, lanes - 1, 1), pltpu.roll(t, 1, 1))
    return a * cosine + (swapped if back else swapped * sine)


def tile_lanes(a, times):
    return jnp.concatenate([a] * times, axis=1) if times > 1 else a


def flat2(a):
    return a.reshape(-1, a.shape[-1])


def gelu_parts(pre):
    root = 0.7978845608028654
    square = pre * pre
    t = jnp.tanh(root * pre * (1.0 + 0.044715 * square))
    hidden = 0.5 * pre * (1.0 + t)
    slope = 0.5 * (1.0 + t) + 0.5 * pre * (1.0 - t * t) * root * (1.0 + 0.134145 * square)
    return hidden, slope


def block_kernel(
    p,
    stream,
    cotangent,
    mixing,
    merging,
    expand,
    shrink,
    small_own,
    length,
    cos_ref,
    sin_ref,
    res_out,
    sg_out,
    gmix_out,
    gmer_out,
    gexp_out,
    gshr_out,
    gsmall_out,
    wa,
    wb,
    wc,
    ws,
    x,
    g,
    normed,
    lanes,
    out,
    dnorm,
    small,
    trade,
    sib_a,
    sib_b,
    sib_c,
    sib_s,
    slot_a,
    slot_b,
    slot_c,
    slot_s,
    ag_send,
    ag_recv,
    as_send,
    as_recv,
    rs_send,
    rs_recv,
    ss_send,
    ss_recv,
    x_send,
    x_recv,
    own_sem,
    sw_mix,
    sw_exp,
    sw_small,
    mer,
    keep_exp,
    sw_send,
    sw_recv,
    sh_send,
    sh_recv,
):
    n, C, D, W, CW, rq, q = p.n, p.C, p.D, p.W, p.CW, p.rq, p.q
    SD = BF if rq % 16 == 0 else F32
    m = n // 2
    half = m // 2
    blocks = p.rows // BLOCK
    pairs = W // 128
    groups = CW // 128
    at_q, at_k, at_v, at_att, at_da = (t * pairs for t in range(5))
    at_hid, at_slope = 0, C * groups
    d = lax.axis_index("dp")
    b = lax.axis_index("branch")
    core = lax.rem(d, 2)
    chip = d // 2
    ring = jnp.where(lax.rem(chip, 2) == 0, chip // 2, m - 1 - chip // 2)
    step = 1 - 2 * core

    def around(k):
        pos = lax.rem(ring + step * k + m, m)
        return jnp.where(pos < half, 2 * pos, 2 * (m - 1 - pos) + 1)

    ahead = (2 * around(1) + core, b)
    behind = (2 * around(-1) + core, b)
    sibling = (d + step, b)
    partner = (d, 1 - b)
    ways = (ahead, behind)

    sources = [(mixing, t * D, t * rq, rq) for t in range(3)]
    sources += [(expand, t * D, (3 + t) * rq, rq) for t in range(p.FF // D)]
    sources += [(merging, 0, 7 * rq, p.rr), (shrink, 0, 8 * rq, p.hb)]
    loads = [
        pltpu.make_async_copy(
            ref.at[:, pl.ds(column, D)], dnorm.at[pl.ds(row, count)], own_sem.at[2 + t]
        )
        for t, (ref, column, row, count) in enumerate(sources)
    ]
    for load in loads:
        load.start()
    barrier = pltpu.get_barrier_semaphore()
    for other in (ahead, behind, sibling, partner):
        pl.semaphore_signal(barrier, inc=1, device_id=other, device_id_type=MESH)
    rank, origin = 2 * d + b, n * b + d
    merge_to = (lax.rem(rank, n), rank // n)
    merge_from = (origin // 2, lax.rem(origin, 2))
    moves = d != b * (n - 1)

    @pl.when(moves)
    def _():
        for other in (merge_to, merge_from):
            pl.semaphore_signal(barrier, inc=1, device_id=other, device_id_type=MESH)
        pl.semaphore_wait(barrier, 6)

    @pl.when(jnp.logical_not(moves))
    def _():
        pl.semaphore_wait(barrier, 4)


    def remote(src, dst, send, recv, to):
        return pltpu.make_async_remote_copy(
            src_ref=src, dst_ref=dst, send_sem=send, recv_sem=recv, device_id=to, device_id_type=MESH
        )

    own_rows = pl.ds(pl.multiple_of(b * p.own_rows, p.own_rows), p.own_rows)
    their_rows = pl.ds(pl.multiple_of((1 - b) * p.own_rows, p.own_rows), p.own_rows)

    def gather_ref(k):
        return wa if k == 0 else wb if k == 1 else wc.at[k - 2]

    def last_hop(way):
        return half - way

    def gather_copy(k, way, hop):
        shard = gather_ref(k).at[around((1 - hop) * (1 - 2 * way)), core]
        return remote(shard, shard, ag_send.at[k, way, hop], ag_recv.at[k, way, hop], ways[way])

    def gather_arrival(k, way, hop):
        shard = gather_ref(k).at[around(-hop * (1 - 2 * way)), core]
        return remote(shard, shard, ag_send.at[k, way, hop], ag_recv.at[k, way, hop], ways[way])

    def gather_sibling(k, whose):
        part = gather_ref(k).at[:, whose]
        return remote(part, part, as_send.at[k], as_recv.at[k], sibling)

    def gather_share(k, way, hop, arriving):
        shift = -hop * (1 - 2 * way)
        shard = gather_ref(k)
        shard = shard.at[around(-shift), 1 - core] if arriving else shard.at[around(shift), core]
        return remote(shard, shard, sh_send.at[k, way, hop], sh_recv.at[k, way, hop], sibling)

    def shares():
        hops = [(way, hop) for way in range(2) for hop in range(1, last_hop(way) + 1)]
        return [(0, 0)] + hops

    def gather_start(k):
        for way in range(2):
            gather_copy(k, way, 1).start()
        if k < 2:
            gather_share(k, 0, 0, False).start()

    def gather_event(k, hop):
        for way in range(2):
            if hop <= last_hop(way):
                gather_arrival(k, way, hop).wait_recv()
                if hop < last_hop(way):
                    gather_copy(k, way, hop + 1).start()
                if k < 2:
                    gather_share(k, way, hop, False).start()
        if hop == half and k >= 2:
            gather_sibling(k, core).start()

    def gather_ready(k):
        if k >= 2:
            gather_sibling(k, 1 - core).wait_recv()
            return
        for way, hop in shares():
            gather_share(k, way, hop, True).wait_recv()

    def gather_done(k):
        for way in range(2):
            for hop in range(1, last_hop(way) + 1):
                gather_copy(k, way, hop).wait_send()
        if k >= 2:
            gather_sibling(k, core).wait_send()
            return
        for way, hop in shares():
            gather_share(k, way, hop, False).wait_send()

    def scatter_refs(k):
        if k == 0:
            return wa, sib_a, slot_a, 6 * rq
        if k == 1:
            return wb, sib_b, slot_b, 2 * p.mr
        if k < C + 2:
            return wc.at[k - 2], sib_c.at[k - 2], slot_c.at[k - 2], p.c_rows
        return ws, sib_s, slot_s, 16

    def swap_copy(ref, src, dst, sem):
        return remote(ref.at[src], ref.at[dst], sw_send.at[sem], sw_recv.at[sem], partner)

    def exp_back(j):
        cut = pl.ds(j * rq, rq)
        return remote(
            sw_exp.at[0, cut], sw_exp.at[2, cut], sw_send.at[7 + j], sw_recv.at[7 + j], partner
        )

    def mer_back():
        return remote(mer.at[0], mer.at[1], sw_send.at[5], sw_recv.at[5], merge_from)

    def pair(upper, lower):
        return jnp.where(b == 0, upper, lower), jnp.where(b == 0, lower, upper)

    def half_lanes(t, which):
        return pl.ds(pl.multiple_of(t * D + which * W, W), W)

    def scatter_result(k, total):
        if k == 0:
            for t in range(3):
                upper = total[2 * t * rq : (2 * t + 1) * rq]
                keep, give = pair(upper, total[(2 * t + 1) * rq : (2 * t + 2) * rq])
                gmix_out[:, half_lanes(t, b)] = keep
                sw_mix[0, t * rq : (t + 1) * rq] = give.astype(SD)
            swap_copy(sw_mix, 0, 2, 4).start()
        elif k == 1:
            mer[0] = total.astype(BF)

            @pl.when(moves)
            def _():
                mer_back().start()

        elif k < C + 2:
            j = k - 2
            keep, give = pair(total[:rq], total[rq : 2 * rq])
            keep_exp[j * rq : (j + 1) * rq] = keep
            sw_exp[0, j * rq : (j + 1) * rq] = give.astype(SD)
            exp_back(j).start()
            for t in range(p.wb):
                part = total[2 * rq + t * q : 2 * rq + (t + 1) * q]
                gshr_out[j * q : (j + 1) * q, t * CW : (t + 1) * CW] = part
        else:
            sw_small[0] = total
            swap_copy(sw_small, 0, 2, 6).start()

    def scatter_sibling(k):
        whole, sib, _, rows = scatter_refs(k)
        src = whole.at[:, 1 - core, pl.ds(0, rows)]
        return remote(src, sib, ss_send.at[k], ss_recv.at[k], sibling)

    def slot_of(way, hop):
        return (hop - 1) if way == 0 else half + hop - 1

    def scatter_copy(k, way, hop):
        whole, _, slots, rows = scatter_refs(k)
        target = around((last_hop(way) + 1 - hop) * (1 - 2 * way))
        src = whole.at[target, core, pl.ds(0, rows)]
        return remote(
            src, slots.at[slot_of(way, hop)], rs_send.at[k, way, hop], rs_recv.at[k, way, hop], ways[way]
        )

    def scatter_event(k, hop):
        whole, sib, slots, rows = scatter_refs(k)
        if hop == 0:
            scatter_sibling(k).start()
            return
        if hop == 1:
            scatter_sibling(k).wait_recv()
        for way in range(2):
            if hop <= last_hop(way):
                target = around((last_hop(way) + 1 - hop) * (1 - 2 * way))
                here = whole.at[target, core, pl.ds(0, rows)]
                total = here[...].astype(F32) + sib[target].astype(F32)
                if hop > 1:
                    scatter_copy(k, way, hop - 1).wait_recv()
                    total = total + slots[slot_of(way, hop - 1)].astype(F32)
                here[...] = total.astype(BF)
                scatter_copy(k, way, hop).start()
        if hop == half + 1:
            total = whole[chip, core, pl.ds(0, rows)].astype(F32) + sib[chip].astype(F32)
            for way in range(2):
                scatter_copy(k, way, last_hop(way)).wait_recv()
                total = total + slots[slot_of(way, last_hop(way))].astype(F32)
            scatter_result(k, total)
            for way in range(2):
                for sent in range(1, last_hop(way) + 1):
                    scatter_copy(k, way, sent).wait_send()
            scatter_sibling(k).wait_send()

    piece = p.own_rows // 2

    def quarter(whose, t):
        return pl.ds(pl.multiple_of(whose * p.own_rows + t * piece, piece), piece)

    def row_copy(kind, t, receiving):
        src, dst = ((stream, x), (cotangent, g))[kind]
        sem = 2 * kind + t
        there = dst.at[quarter(1 - b if receiving else b, t)]
        return remote(src.at[pl.ds(t * piece, piece)], there, x_send.at[sem], x_recv.at[sem], partner)

    keep_x = pltpu.make_async_copy(stream, x.at[own_rows], own_sem.at[0])
    keep_g = pltpu.make_async_copy(cotangent, g.at[own_rows], own_sem.at[1])

    for t in range(3):
        loads[t].wait()
    kept_mix = []
    for t in range(3):
        v = dnorm[t * rq : (t + 1) * rq]
        keep, give = pair(v[:, :W], v[:, W:])
        kept_mix.append(keep)
        sw_mix[0, t * rq : (t + 1) * rq] = give.astype(SD)
    swap_copy(sw_mix, 0, 1, 0).start()
    sw_small[0] = small_own[...]
    swap_copy(sw_small, 0, 1, 1).start()
    row_copy(0, 0, False).start()
    for load in loads[3:]:
        load.wait()
    mer[0] = jnp.zeros((2 * p.mr, W), BF)
    own_merge = dnorm[7 * rq : 7 * rq + p.rr].astype(BF)
    for t in range(2):
        mer[0, t * p.mr : t * p.mr + p.rr] = own_merge[:, t * W : (t + 1) * W]
    mer_there = (merge_to[0] // 2, lax.rem(merge_to[0], 2))

    def mer_copy(slot):
        return remote(mer.at[0], wb.at[slot], sw_send.at[3], sw_recv.at[3], merge_to)

    @pl.when(moves)
    def _():
        mer_copy(mer_there).start()

    @pl.when(jnp.logical_not(moves))
    def _():
        wb[chip, core] = mer[0]

    swap_copy(sw_mix, 0, 1, 0).wait_recv()
    swap_copy(sw_small, 0, 1, 1).wait_recv()
    for t in range(3):
        got = sw_mix[1, t * rq : (t + 1) * rq].astype(F32)
        both_halves = jnp.concatenate(pair(kept_mix[t], got), axis=0).astype(BF)
        wa[chip, core, 2 * t * rq : 2 * (t + 1) * rq] = both_halves
    wa[chip, core, 6 * rq : 6 * rq + 16] = (sw_small[0] + sw_small[1]).astype(BF)
    gather_start(0)

    @pl.when(moves)
    def _():
        mer_copy((chip, core)).wait_recv()

    gather_start(1)
    per_lane = 128 // q

    def pieces(fetch, width):
        spot = lax.broadcasted_iota(jnp.int32, (width, 128), 1) // q
        result = None
        for e in range(per_lane):
            block, at = fetch(e)
            shift = (e * q - at) % 128
            block = pltpu.roll(block, shift, 1) if shift else block
            result = block if e == 0 else jnp.where(spot == e, block, result)
        return result

    def to_plane(block_at, width, j, plane):
        def column(o):
            def fetch(e):
                start = (2 * (o * per_lane + e) + plane) * p.hb + j * q
                return block_at(start // 128), start % 128

            return pieces(fetch, width)

        return jnp.concatenate([column(o) for o in range(groups)], axis=1)

    def from_plane(block_at, width):
        def column(c):
            def fetch(e):
                start = c * 128 + e * q
                unit_block = start // p.hb
                lane = (unit_block // 2) * q
                block = block_at(unit_block % 2, (start % p.hb) // q, lane // 128)
                return block, lane % 128

            return pieces(fetch, width)

        return [column(c) for c in range(p.FF // 128)]

    wide_blocks = D // 128

    def expand_block(c):
        at = (3 + c // wide_blocks) * rq
        lane = (c % wide_blocks) * 128
        return dnorm[at : at + rq, lane : lane + 128]

    for j in range(C):
        keep, give = pair(to_plane(expand_block, rq, j, 0), to_plane(expand_block, rq, j, 1))
        keep_exp[j * rq : (j + 1) * rq] = keep
        sw_exp[0, j * rq : (j + 1) * rq] = give.astype(SD)
    swap_copy(sw_exp, 0, 1, 2).start()

    @pl.when(b == 0)
    def _():
        row_copy(0, 1, False).start()
        row_copy(1, 0, False).start()

    @pl.when(b == 1)
    def _():
        row_copy(1, 0, False).start()
        row_copy(0, 1, False).start()

    row_copy(1, 1, False).start()
    keep_x.start()
    keep_g.start()
    for j in range(C):
        for t in range(p.wb):
            at = 8 * rq + j * q
            piece_rows = dnorm[at : at + q, t * CW : (t + 1) * CW].astype(BF)
            wc[j, chip, core, 2 * rq + t * q : 2 * rq + (t + 1) * q] = piece_rows
    def chunk_shards():
        swap_copy(sw_exp, 0, 1, 2).wait_recv()
        for j in range(C):
            got = sw_exp[1, j * rq : (j + 1) * rq].astype(F32)
            both_halves = jnp.concatenate(pair(keep_exp[j * rq : (j + 1) * rq], got), axis=0)
            wc[j, chip, core, : 2 * rq] = both_halves.astype(BF)

    out[...] = jnp.zeros((p.rows, D), F32)
    for hop in range(1, half + 1):
        gather_event(0, hop)
        gather_event(1, hop)
        if hop == half - 1:
            chunk_shards()
            gather_start(2)
    for j in range(1, C):
        gather_start(2 + j)
    swap_copy(sw_mix, 0, 1, 0).wait_send()
    swap_copy(sw_small, 0, 1, 1).wait_send()
    swap_copy(sw_exp, 0, 1, 2).wait_send()

    @pl.when(moves)
    def _():
        mer_copy(mer_there).wait_send()


    def weight(t):
        return flat2(wa[:, :, t * 2 * rq : (t + 1) * 2 * rq, :])

    def merge_weight(t):
        whole = wb[:, :, t * p.mr : (t + 1) * p.mr, :]
        if p.mr == p.rr:
            return flat2(whole)
        whole = whole.astype(F32).reshape(n, p.mr, W)[:, : p.rr]
        return whole.reshape(W, W).astype(BF)

    def wide(row):
        return jnp.concatenate([small[row : row + 1], small[row + 1 : row + 2]], axis=1)

    def unit(rows):
        v = x[rows].astype(F32)
        centred = v - jnp.mean(v, axis=1, keepdims=True)
        inverse = lax.rsqrt(jnp.mean(centred * centred, axis=1, keepdims=True) + norm_eps)
        return centred * inverse, inverse

    def rows_of(i):
        return pl.ds(pl.multiple_of(i * BLOCK, BLOCK), BLOCK)

    def project(i):
        rows = rows_of(i)
        z, _ = unit(rows)
        nb = (z * wide(0) + wide(2)).astype(BF)
        normed[rows] = nb
        cosine = tile_lanes(cos_ref[rows], pairs)
        sine = tile_lanes(sin_ref[rows], pairs)
        query = (turned(dot(nb, weight(0)), cosine, sine, False) * HEAD**-0.5).astype(BF)
        key = turned(dot(nb, weight(1)), cosine, sine, False).astype(BF)
        value = dot(nb, weight(2)).astype(BF)
        for t in range(pairs):
            cut = slice(t * 128, (t + 1) * 128)
            lanes[at_q + t, rows] = query[:, cut]
            lanes[at_k + t, rows] = key[:, cut]
            lanes[at_v + t, rows] = value[:, cut]

    def gradient(i):
        rows = rows_of(i)
        position = lax.broadcasted_iota(jnp.int32, (BLOCK, D), 0) + i * BLOCK
        gb = jnp.where(position < length[0], g[rows].astype(F32), 0.0).astype(BF)
        g[rows] = gb
        da = (dot_right(gb[:, :W], merge_weight(0)) + dot_right(gb[:, W:], merge_weight(1))).astype(BF)
        for t in range(pairs):
            lanes[at_da + t, rows] = da[:, t * 128 : (t + 1) * 128]

    def each(body, start, count):
        def run(i, carry):
            body(start + i)
            return carry

        lax.fori_loop(0, count, run, 0)

    keep_x.wait()
    keep_g.wait()
    gather_ready(0)
    small[:16] = jnp.sum(wa[:, :, 6 * rq :, :].reshape(n, 16, W).astype(F32), axis=0)
    first_bias, plane_bias, plane_grad = 2 * D // W, 32, 40

    def bias_block(c):
        row, lane = first_bias + c * 128 // W, c * 128 % W
        return jnp.broadcast_to(small[row : row + 1, lane : lane + 128], (8, 128))

    for j in range(C):
        mine, _ = pair(to_plane(bias_block, 8, j, 0), to_plane(bias_block, 8, j, 1))
        for t in range(CW // W):
            row = plane_bias + j * CW // W + t
            small[row : row + 1] = mine[:1, t * W : (t + 1) * W]
    part = blocks // 2
    each(project, b * part, part)
    gather_ready(1)
    each(gradient, b * part, part)

    @pl.when(b == 1)
    def _():
        row_copy(0, 0, True).wait_recv()
        row_copy(0, 1, True).wait_recv()
        each(project, 0, part)

    def spread(items, count, first=0):
        return [items[len(items) * t // count : len(items) * (t + 1) // count] for t in range(count)]

    events = []
    for hop in range(1, half + 1):
        events += [(2 + j, hop) for j in range(C)]
    attend_slots = spread(events[: len(events) * ATTEND_SHARE // 16], blocks * pairs)
    merge_events = events[len(events) * ATTEND_SHARE // 16 :]

    def attend(i, t):
        lane = lax.broadcasted_iota(jnp.int32, (BLOCK, 128), 1)
        rows = slice(i * BLOCK, (i + 1) * BLOCK)
        width = (i + 1) * BLOCK
        qb, dab = lanes[at_q + t, rows], lanes[at_da + t, rows]
        keys, values = lanes[at_k + t, :width], lanes[at_v + t, :width]
        zero = jnp.zeros_like(qb)
        mixed = []
        dquery = []
        dkey = jnp.zeros((width, 128), F32)
        dvalue = jnp.zeros((width, 128), F32)
        for h in range(2):
            mine = (lane < HEAD) if h == 0 else (lane >= HEAD)
            qm = jnp.where(mine, qb, zero)
            dm = jnp.where(mine, dab, zero)
            scores = dot_right(qm, keys)
            down = lax.broadcasted_iota(jnp.int32, (BLOCK, BLOCK), 0)
            over = lax.broadcasted_iota(jnp.int32, (BLOCK, BLOCK), 1)
            edge = jnp.where(down >= over, scores[:, width - BLOCK :], masked_score)
            scores = jnp.concatenate([scores[:, : width - BLOCK], edge], axis=1) if i else edge
            weights = jnp.exp(scores - jnp.max(scores, axis=1, keepdims=True))
            weights = weights * (1.0 / jnp.sum(weights, axis=1, keepdims=True))
            rounded = weights.astype(BF)
            dweights = dot_right(dm, values)
            delta = jnp.sum(weights * dweights, axis=1, keepdims=True)
            dscores = (weights * (dweights - delta)).astype(BF)
            mixed.append(dot(rounded, values))
            dquery.append(dot(dscores, keys))
            dvalue = dvalue + dot_left(rounded, dm)
            dkey = dkey + dot_left(dscores, qm)
        first = lane < HEAD
        position = lax.broadcasted_iota(jnp.int32, (BLOCK, 128), 0) + i * BLOCK
        whole = jnp.where(first, mixed[0], mixed[1])
        lanes[at_att + t, rows] = jnp.where(position < length[0], whole, 0.0).astype(BF)
        dq = jnp.where(first, dquery[0], dquery[1]) * HEAD**-0.5
        lanes[at_q + t, rows] = turned(dq, cos_ref[rows], sin_ref[rows], True).astype(BF)
        out[:width, head_lanes(t, 0)] += dkey
        out[:width, head_lanes(t, 1)] += dvalue

    def head_lanes(t, which):
        return pl.ds(pl.multiple_of(which * W + t * 128, 128), 128)

    def attention(it, carry):
        stage, t = it // pairs, lax.rem(it, pairs)
        now = lax.rem(stage + b * part, blocks)

        @pl.when((t == 0) & (b == 0) & (stage >= part))
        def _():
            for u in range(2):

                @pl.when(stage == part + u * (part // 2))
                def _(u=u):
                    row_copy(0, u, True).wait_recv()
                    row_copy(1, u, True).wait_recv()
                    each(project, part + u * (part // 2), part // 2)
                    each(gradient, part + u * (part // 2), part // 2)

        @pl.when((t == 0) & (b == 1) & (stage == part))
        def _():
            row_copy(1, 0, True).wait_recv()
            row_copy(1, 1, True).wait_recv()
            each(gradient, 0, part)

        for i in range(blocks):

            @pl.when(now == i)
            def _(i=i):
                attend(i, t)

        @pl.when(stage == blocks - 1)
        def _():
            dk = out[:, head_lanes(t, 0)]
            lanes[at_k + t] = turned(dk, cos_ref[...], sin_ref[...], True).astype(BF)
            lanes[at_v + t] = out[:, head_lanes(t, 1)].astype(BF)

        for slot, todo in enumerate(attend_slots):
            if todo:

                @pl.when(it == slot)
                def _(todo=todo):
                    for k, hop in todo:
                        gather_event(k, hop)

        return carry

    lax.fori_loop(0, blocks * pairs, attention, 0)

    def side(at, rows, count=pairs):
        return jnp.concatenate([lanes[at + t, rows] for t in range(count)], axis=1)

    def merge(i, carry):
        rows = rows_of(i)
        total = dot_right(side(at_q, rows), weight(0))
        total = total + dot_right(side(at_k, rows), weight(1))
        dnorm[rows] = total + dot_right(side(at_v, rows), weight(2))
        return carry

    lax.fori_loop(0, blocks, merge, 0)
    for k, hop in merge_events[: len(merge_events) // 2]:
        gather_event(k, hop)
    gather_done(0)
    every = slice(0, p.rows)
    chips = BLOCK // (4 * rq)

    def mix_grads(i, carry):
        left = normed[:, rows_of(i)]
        where = pl.ds(i * chips, chips)
        for t in range(3):
            res = dot_left(left, side(t * pairs, every)).astype(BF)
            wa[where, :, t * 2 * rq : (t + 1) * 2 * rq, :] = res.reshape(chips, 2, 2 * rq, W)
        return carry

    lax.fori_loop(0, D // BLOCK, mix_grads, 0)
    scatter_event(0, 0)
    for k, hop in merge_events[len(merge_events) // 2 :]:
        gather_event(k, hop)

    def attend_out(i, carry):
        rows = rows_of(i)
        ab = side(at_att, rows)
        out[rows, :W] = dot(ab, merge_weight(0))
        out[rows, W:] = dot(ab, merge_weight(1))
        return carry

    lax.fori_loop(0, blocks, attend_out, 0)
    gather_done(1)
    merged = BLOCK // (2 * p.rr)
    for i in range(W // BLOCK):
        left = side(at_att + 2 * i, every, 2)
        for t in range(2):
            res = dot_left(left, g[:, t * W : (t + 1) * W]).reshape(merged, 2, p.rr, W)
            if p.mr != p.rr:
                res = jnp.concatenate([res, jnp.zeros((merged, 2, p.mr - p.rr, W), F32)], axis=2)
            wb[i * merged : (i + 1) * merged, :, t * p.mr : (t + 1) * p.mr, :] = res.astype(BF)
    scatter_event(1, 0)

    order = [(0, j) for j in range(C)]
    for j in range(C):
        if j < C - LATE:
            order += [(1, j), (2, j)]
    order += [(1, j) for j in range(C - LATE, C)] + [(2, j) for j in range(C - LATE, C)]
    fore_at, back_at, grad_at = ({}, {}, {})
    total_slots = 0
    for kind, j in order:
        (fore_at, back_at, grad_at)[kind][j] = total_slots
        total_slots += 2 if kind == 2 else blocks
    timed = []
    pace = 4.0 / half
    for hop in range(1, half + 2):
        timed += [(AB_START + (hop - 1) * AB_STEP * pace, k, hop) for k in range(2)]
        for j in range(C):
            begin = grad_at[j] + 2 + C_START
            timed.append((begin + (hop - 1) * C_STEP * pace, 2 + j, hop))
    timed.sort()
    slots = [[e[1:] for e in timed if t <= e[0] < t + 1] for t in range(total_slots)]
    leftover = [e[1:] for e in timed if e[0] >= total_slots]

    def run_slot(slot):
        for k, hop in slots[slot]:
            scatter_event(k, hop)

    def run_when(i, start):
        for i0 in range(blocks):
            if slots[start + i0]:

                @pl.when(i == i0)
                def _(i0=i0):
                    run_slot(start + i0)

    def hidden_bias(j):
        at = plane_bias + j * CW // W
        return jnp.concatenate([small[at + t : at + t + 1] for t in range(CW // W)], axis=1)

    def shrink_weight(j, t):
        return flat2(wc[j, :, :, 2 * rq + t * q : 2 * rq + (t + 1) * q, :])

    last = (2 * D + p.FF) // W
    give_out = remote(res_out, trade.at[0], x_send.at[4], x_recv.at[4], partner)
    give_dn = remote(res_out, trade.at[1], x_send.at[5], x_recv.at[5], partner)

    def forward(j):
        gather_ready(2 + j)

        def feed(i, carry):
            rows = rows_of(i)
            pre = dot(normed[rows], flat2(wc[j, :, :, : 2 * rq, :])) + hidden_bias(j)
            hid, slope = gelu_parts(pre)
            hid, slope = hid.astype(BF), slope.astype(BF)
            for t in range(groups):
                lanes[at_hid + j * groups + t, rows] = hid[:, t * 128 : (t + 1) * 128]
                lanes[at_slope + j * groups + t, rows] = slope[:, t * 128 : (t + 1) * 128]
            for t in range(p.wb):
                out[rows, t * CW : (t + 1) * CW] += dot(hid, shrink_weight(j, t))
            run_when(i, fore_at[j])
            return carry

        lax.fori_loop(0, blocks, feed, 0)

    def backward(j):

        def back(i, carry):
            rows = rows_of(i)
            gb = g[rows]
            dhid = dot_right(gb[:, :CW], shrink_weight(j, 0))
            for t in range(1, p.wb):
                dhid = dhid + dot_right(gb[:, t * CW : (t + 1) * CW], shrink_weight(j, t))
            dp = (dhid * side(at_slope + j * groups, rows, groups).astype(F32)).astype(BF)
            for t in range(groups):
                lanes[at_slope + j * groups + t, rows] = dp[:, t * 128 : (t + 1) * 128]
            dnorm[rows] += dot_right(dp, flat2(wc[j, :, :, : 2 * rq, :]))
            run_when(i, back_at[j])
            return carry + jnp.sum(dp.astype(F32), axis=0, keepdims=True)

        bias_grad = lax.fori_loop(0, blocks, back, jnp.zeros((1, CW), F32))
        for t in range(CW // W):
            at = plane_grad + j * CW // W + t
            small[at : at + 1] = bias_grad[:, t * W : (t + 1) * W]

    def gradients(j):
        gather_done(2 + j)

        def expand_grads(i, carry):
            res = dot_left(normed[:, rows_of(i)], side(at_slope + j * groups, every, groups)).astype(BF)
            wc[j, pl.ds(i * chips, chips), :, : 2 * rq, :] = res.reshape(chips, 2, 2 * rq, CW)
            return carry

        lax.fori_loop(0, D // BLOCK, expand_grads, 0)
        run_slot(grad_at[j])
        per = BLOCK // (2 * q)

        def shrink_grads(i, carry):
            left = side(at_hid + j * groups + 2 * i, every, 2)
            for t in range(p.wb):
                res = dot_left(left, g[:, t * CW : (t + 1) * CW]).astype(BF)
                cut = slice(2 * rq + t * q, 2 * rq + (t + 1) * q)
                wc[j, pl.ds(i * per, per), :, cut, :] = res.reshape(per, 2, q, CW)
            return carry

        lax.fori_loop(0, CW // BLOCK, shrink_grads, 0)
        scatter_event(2 + j, 0)
        run_slot(grad_at[j] + 1)

    for kind, j in order:
        (forward, backward, gradients)[kind](j)
        if (kind, j) == (0, C - 1):
            res_out[...] = out[their_rows].astype(BF)
            give_out.start()
        if (kind, j) == (1, C - 1):
            give_out.wait_send()
            res_out[...] = dnorm[their_rows].astype(BF)
            give_dn.start()

    def small_gradients():
        def vector_grads(i, carry):
            rows = rows_of(i)
            z, _ = unit(rows)
            dn = dnorm[rows]
            gain = carry[0] + jnp.sum(dn * z, axis=0, keepdims=True)
            shift = carry[1] + jnp.sum(dn, axis=0, keepdims=True)
            return gain, shift, carry[2] + jnp.sum(g[rows].astype(F32), axis=0, keepdims=True)

        zero_row = jnp.zeros((1, D), F32)
        sums = lax.fori_loop(0, blocks, vector_grads, (zero_row, zero_row, zero_row))
        tail_grad = jnp.where(b == 0, sums[2], 0.0)

        def grad_block(plane, j, o):
            at = j * CW + o * 128
            row, lane = plane_grad + at // W, at % W
            v = jnp.broadcast_to(small[row : row + 1, lane : lane + 128], (8, 128))
            return jnp.where(b == plane, v, 0.0)

        for c, v in enumerate(from_plane(grad_block, 8)):
            row, lane = 16 + first_bias + c * 128 // W, c * 128 % W
            small[row : row + 1, lane : lane + 128] = v[:1]
        for at, row in ((0, sums[0]), (2, sums[1]), (last, tail_grad)):
            small[16 + at : 17 + at] = row[:, :W]
            small[17 + at : 18 + at] = row[:, W:]
        small[16 + last + 2 : 32] = jnp.zeros((14 - last, W), F32)
        ws[...] = jnp.broadcast_to(small[16:32].astype(BF)[None, None], (m, 2, 16, W))
        scatter_event(C + 2, 0)

    def finish_all():
        small_rows = p.own_rows // blocks
        give_out.wait_recv()
        give_dn.wait_recv()
        give_dn.wait_send()

        def finish_rows(i, carry):
            local = pl.ds(pl.multiple_of(i * small_rows, small_rows), small_rows)
            rows = pl.ds(pl.multiple_of(b * p.own_rows + i * small_rows, small_rows), small_rows)
            z, inverse = unit(rows)
            tail = wide(last)
            total = out[rows] + trade[0, local].astype(F32) + tail
            res_out[local] = (x[rows].astype(F32) + total).astype(BF)
            du = (dnorm[rows] + trade[1, local].astype(F32)) * wide(0)
            back = du - jnp.mean(du, axis=1, keepdims=True) - z * jnp.mean(du * z, axis=1, keepdims=True)
            sg_out[local] = g[rows].astype(F32) + inverse * back
            return carry

        lax.fori_loop(0, blocks, finish_rows, 0)

    small_hop = 0
    for k, hop in leftover:
        if k == C + 1 and hop == half + 1:
            finish_all()
        scatter_event(k, hop)
        if k == C + 1:
            if hop == 1:
                small_gradients()
            else:
                small_hop += 1
                scatter_event(C + 2, small_hop)
    scatter_event(C + 2, half + 1)

    for kind in range(2):
        for t in range(2):
            row_copy(kind, t, False).wait_send()
    swap_copy(sw_mix, 0, 2, 4).wait()
    for t in range(3):
        gmix_out[:, half_lanes(t, 1 - b)] = sw_mix[2, t * rq : (t + 1) * rq].astype(F32)

    @pl.when(moves)
    def _():
        mer_back().wait_send()
        remote(mer.at[0], mer.at[1], sw_send.at[5], sw_recv.at[5], merge_to).wait_recv()

    @pl.when(jnp.logical_not(moves))
    def _():
        mer[1] = mer[0]

    for t in range(2):
        merged_rows = mer[1, t * p.mr : (t + 1) * p.mr].astype(F32)
        gmer_out[:, t * W : (t + 1) * W] = merged_rows[: p.rr]
    for j in range(C):
        exp_back(j).wait()

    def summed_block(plane, j, o):
        rows, cols = slice(j * rq, (j + 1) * rq), slice(o * 128, (o + 1) * 128)
        return jnp.where(b == plane, keep_exp[rows, cols], sw_exp[2, rows, cols].astype(F32))

    for c, v in enumerate(from_plane(summed_block, rq)):
        gexp_out[:, c * 128 : (c + 1) * 128] = v
    swap_copy(sw_small, 0, 2, 6).wait()
    gsmall_out[...] = sw_small[0] + sw_small[2]


def core(p, stream, cotangent, lengths, mixing, merging, expand, shrink, small_own):
    n, C, D, W, CW, rq = p.n, p.C, p.D, p.W, p.CW, p.rq
    m = n // 2
    half = m // 2
    hops = 2 * half - 1
    rows = p.rows
    a_rows = 6 * rq + 16
    b_rows = 2 * p.mr
    cosine, sine = (jnp.asarray(table) for table in rope_tables(rows))
    vmem = pl.BlockSpec(memory_space=pltpu.VMEM)
    hbm = pl.BlockSpec(memory_space=pl.ANY)
    dma = pltpu.SemaphoreType.DMA
    V = pltpu.VMEM
    SD = BF if rq % 16 == 0 else F32
    scratch = [
        V((m, 2, a_rows, W), BF),
        V((m, 2, b_rows, W), BF),
        V((C, m, 2, p.c_rows, CW), BF),
        V((m, 2, 16, W), BF),
        V((rows, D), BF),
        V((rows, D), BF),
        V((rows, D), BF),
        V((max(5 * W, 2 * p.C * CW) // 128, rows, 128), BF),
        V((rows, D), F32),
        V((rows, D), F32),
        V((48, W), F32),
        V((2, p.own_rows, D), BF),
        V((m, 6 * rq, W), BF),
        V((m, b_rows, W), BF),
        V((C, m, p.c_rows, CW), BF),
        V((m, 16, W), BF),
        V((hops, 6 * rq, W), BF),
        V((hops, b_rows, W), BF),
        V((C, hops, p.c_rows, CW), BF),
        V((hops, 16, W), BF),
        dma((C + 2, 2, half + 1)),
        dma((C + 2, 2, half + 1)),
        dma((C + 2,)),
        dma((C + 2,)),
        dma((C + 3, 2, half + 1)),
        dma((C + 3, 2, half + 1)),
        dma((C + 3,)),
        dma((C + 3,)),
        dma((6,)),
        dma((6,)),
        dma((7 + p.FF // D,)),
        V((3, 3 * rq, W), SD),
        V((3, C * rq, CW), SD),
        V((3, 16, W), F32),
        V((2, b_rows, W), BF),
        V((C * rq, CW), F32),
        dma((7 + C,)),
        dma((7 + C,)),
        dma((2, 2, half + 1)),
        dma((2, 2, half + 1)),
    ]
    shapes = (
        jax.ShapeDtypeStruct((p.own_rows, D), BF),
        jax.ShapeDtypeStruct((p.own_rows, D), F32),
        jax.ShapeDtypeStruct((rq, 3 * D), F32),
        jax.ShapeDtypeStruct((p.rr, D), F32),
        jax.ShapeDtypeStruct((rq, p.FF), F32),
        jax.ShapeDtypeStruct((p.hb, D), F32),
        jax.ShapeDtypeStruct((16, W), F32),
    )
    flops = 2 * rows * D * (6 * p.FF // 2 + 9 * W + 3 * W) + 12 * rows * rows * W
    return pl.pallas_call(
        functools.partial(block_kernel, p),
        out_shape=shapes,
        in_specs=[hbm] * 6 + [vmem, pl.BlockSpec(memory_space=pltpu.SMEM), vmem, vmem],
        out_specs=tuple(vmem for _ in shapes),
        scratch_shapes=scratch,
        compiler_params=pltpu.CompilerParams(
            collective_id=0, has_side_effects=True, vmem_limit_bytes=63 * 1024 * 1024
        ),
        cost_estimate=pl.CostEstimate(flops=flops, bytes_accessed=8 << 20, transcendentals=0),
    )(stream, cotangent, mixing, merging, expand, shrink, small_own, lengths, cosine, sine)


def local(n, stream, cotangent, lengths, steps_taken, learning_rates, *params):
    masters, momenta, variances = params[:6], params[6:12], params[12:]
    p = Plan(n, stream, *masters)
    linear = lax.axis_index("dp") * 2 + lax.axis_index("branch")
    vectors, offsets = masters[4], masters[5]
    small = jnp.zeros((16 * p.W,), F32)
    for row in range(2):
        small = lax.dynamic_update_slice(small, vectors[row], (row * p.D + linear * p.vc,))
    small = lax.dynamic_update_slice(small, offsets, (2 * p.D + linear * p.ow,))
    residual, stream_grad, *grads, small = core(
        p, stream, cotangent, lengths, *masters[:4], small.reshape(16, p.W)
    )
    small = small.reshape(-1)
    rows = [
        lax.dynamic_slice(small, (row * p.D + linear * p.vc,), (p.vc,)) for row in range(2)
    ]
    grads.append(jnp.stack(rows))
    grads.append(lax.dynamic_slice(small, (2 * p.D + linear * p.ow,), (p.ow,)))
    count = steps_taken[0].astype(F32)
    outs = [residual, stream_grad]
    for k in range(6):
        decay = decay_rate if k < 4 else 0.0
        outs.extend(
            adam_update(
                masters[k], grads[k], momenta[k], variances[k], learning_rates[k], count, decay
            )
        )
    return tuple(outs)


def solution(mesh):
    rows = P(("dp", "branch"), None)
    cols = P(None, ("dp", "branch"))
    flat = P(("dp", "branch"))
    six = (rows, rows, rows, rows, cols, flat)
    return jax.shard_map(
        functools.partial(local, mesh.shape["dp"]),
        mesh=mesh,
        in_specs=(rows, rows, P("dp"), P(), P()) + six * 3,
        out_specs=(rows, rows) + sum(((s,) * 4 for s in six), ()),
        check_vma=False,
    )
```

profile of v0, /device:TPU:0, one launch (start us, length us, event | category | flops | bytes accessed | tf_op | source)
XLA Modules:
  0.0 210.1 jit_solution(4381441245555204534)
XLA Ops:
  0.7 0.8 bitcast_dynamic-update-slice_fusion.1
  1.5 0.8 bitcast_dynamic-update-slice_fusion
  2.3 0.9 dynamic_update_slice.11
  3.1 0.6 reshape.67.small_own
  4.4 0.0 copy-start.17
  4.4 0.0 copy-start.10
  4.4 0.0 copy-start.11
  4.4 190.0 %shard_map.440 = (bf16[512,1024]{1,0:T(8,128)(2,1)}, f32[512,1024]{1,0:T(8,128)}, f32[32,3072]{1,0:T(8,128)}, f32[32,1024]{1,0:T(8,128)}, f32[32,4096]{1,0:T(8,1...) custom-call(bf16[512,1024]{1,0:T(8,128)(2,1)} %stream.1, bf16[512,1024]{1,0:T(8,128)(2,1)} %cotangent.1, f32[32,3072]{1,0:T(8,128)} %mixing.1, ...), custom_call_target="tpu_custom_call" | custom-call | flops 45097156608 | bytes 8388608 | tf_op jit(solution)/shard_map/pallas_call | solution.py:1053
  194.4 0.0 copy-start.12
  194.4 0.0 copy-start.13
  194.4 0.0 copy-start.14
  194.5 0.0 copy-start.15
  194.5 0.0 copy-start.2
  194.5 0.0 copy-start.3
  194.5 0.0 copy-start.4
  194.5 0.0 copy-start.9
  195.4 0.0 copy-done.17
  195.4 0.6 fusion.18
  196.0 0.0 copy-done.10
  196.0 0.0 copy-done.11
  196.0 3.0 %fusion.16 = (bf16[32,3072]{1,0:T(8,128)(2,1)}, f32[32,3072]{1,0:T(8,128)}, f32[32,3072]{1,0:T(8,128)}, f32[32,3072]{1,0:T(8,128)}) fusion(f32[32,3072]{1,0:T(8,128)S(1)} %copy-done.10, f32[]{:T(128)} %bitcast.4, f32[]{:T(128)} %bitcast.3, f32[]{:T(128)} %bitcast.2, f32[32,3072]{1,0:T(8,128)} %get-tuple-element.35, f32[32,3072]{1,0:T(8,128)S(1)} %copy-done.11, ...), kind=kLoop, calls=%fused_computation.34 | loop fusion | flops 1572864 | bytes 2949132 | tf_op jit(solution)/shard_map/convert_element_type | solution.py:56
  199.0 0.0 copy-done.12
  199.0 0.0 copy-done.13
  199.0 0.0 copy-done.14
  199.0 0.0 copy-done.15
  199.0 1.5 fusion.14
  200.5 0.0 copy-start.5
  200.5 0.0 copy-start.6
  200.5 0.0 copy-start.7
  200.5 0.0 copy-start.8
  200.5 0.0 copy-done.2
  200.5 0.0 copy-done.3
  200.5 0.0 copy-done.4
  200.5 0.0 copy-done.9
  200.6 2.3 %fusion.12 = (bf16[32,4096]{1,0:T(8,128)(2,1)}, f32[32,4096]{1,0:T(8,128)}, f32[32,4096]{1,0:T(8,128)}, f32[32,4096]{1,0:T(8,128)}) fusion(f32[32,4096]{1,0:T(8,128)S(1)} %copy-done.2, f32[]{:T(128)} %bitcast.4, f32[]{:T(128)} %bitcast.3, f32[]{:T(128)} %bitcast.6, f32[32,4096]{1,0:T(8,128)S(1)} %copy-done.9, f32[32,4096]{1,0:T(8,128)S(1)} %copy-done.3, ...), kind=kLoop, calls=%fused_computation.32 | loop fusion | flops 2097152 | bytes 3932172 | tf_op jit(solution)/shard_map/convert_element_type | solution.py:56
  202.8 0.0 copy-start.16
  202.8 0.0 copy-start.19
  202.8 0.0 copy-start.20
  202.8 0.0 copy-start.21
  202.8 0.0 copy-start.18
  202.8 0.0 copy-start.22
  202.8 0.0 copy-start.23
  202.9 0.0 copy-start.1
  202.9 0.0 copy-done.5
  202.9 0.0 copy-done.6
  202.9 0.0 copy-done.7
  202.9 0.0 copy-done.8
  202.9 0.0 copy-start
  202.9 2.3 %fusion.10 = (bf16[128,1024]{1,0:T(8,128)(2,1)}, f32[128,1024]{1,0:T(8,128)}, f32[128,1024]{1,0:T(8,128)}, f32[128,1024]{1,0:T(8,128)}) fusion(f32[128,1024]{1,0:T(8,128)S(1)} %copy-done.5, f32[]{:T(128)} %bitcast.4, f32[]{:T(128)} %bitcast.3, f32[]{:T(128)} %bitcast.7, f32[128,1024]{1,0:T(8,128)S(1)} %copy-done.8, f32[128,1024]{1,0:T(8,128)S(1)} %copy-done.6, ...), kind=kLoop, calls=%fused_computation.31 | loop fusion | flops 2097152 | bytes 3932172 | tf_op jit(solution)/shard_map/convert_element_type | solution.py:56
  205.2 0.0 copy-done.16
  205.2 0.1 dynamic-slice_bitcast_fusion.1
  205.3 0.0 copy-done.19
  205.3 0.0 copy-done.20
  205.3 0.0 copy-done.21
  205.3 1.2 fusion.8
  206.6 0.0 copy-done.18
  206.6 0.0 copy-done.22
  206.6 0.0 copy-done.23
  206.6 1.2 fusion.6
  207.8 0.0 copy-done.1
  207.8 1.0 copy.59
  208.8 0.0 copy-done
  208.8 1.3 copy.60
  (2 shorter events, 0.0 us)
Async XLA Ops:
  4.4 191.0 %copy-start.17 = (f32[6]{0:T(128)S(1)}, f32[6]{0:T(128)}, u32[]{:S(2)}) copy-start(f32[6]{0:T(128)} %param.29) | copy-start | bytes 76
  4.4 191.6 %copy-start.10 = (f32[32,3072]{1,0:T(8,128)S(1)}, f32[32,3072]{1,0:T(8,128)}, u32[]{:S(2)}) copy-start(f32[32,3072]{1,0:T(8,128)} %mixing.1) | copy-start | bytes 1179652
  4.4 191.6 %copy-start.11 = (f32[32,3072]{1,0:T(8,128)S(1)}, f32[32,3072]{1,0:T(8,128)}, u32[]{:S(2)}) copy-start(f32[32,3072]{1,0:T(8,128)} %param.42) | copy-start | bytes 1179652
  194.4 4.6 %copy-start.12 = (f32[32,1024]{1,0:T(8,128)S(1)}, f32[32,1024]{1,0:T(8,128)}, u32[]{:S(2)}) copy-start(f32[32,1024]{1,0:T(8,128)} %merging.1) | copy-start | bytes 393220
  194.4 4.6 %copy-start.13 = (f32[32,1024]{1,0:T(8,128)S(1)}, f32[32,1024]{1,0:T(8,128)}, u32[]{:S(2)}) copy-start(f32[32,1024]{1,0:T(8,128)} %param.43) | copy-start | bytes 393220
  194.4 4.6 %copy-start.14 = (f32[32,1024]{1,0:T(8,128)S(1)}, f32[32,1024]{1,0:T(8,128)}, u32[]{:S(2)}) copy-start(f32[32,1024]{1,0:T(8,128)} %param.37) | copy-start | bytes 393220
  194.5 4.6 %copy-start.15 = (f32[32,1024]{1,0:T(8,128)S(1)}, f32[32,1024]{1,0:T(8,128)}, u32[]{:S(2)}) copy-start(f32[32,1024]{1,0:T(8,128)} %get-tuple-element.36) | copy-start | bytes 393220
  194.5 6.0 %copy-start.2 = (f32[32,4096]{1,0:T(8,128)S(1)}, f32[32,4096]{1,0:T(8,128)}, u32[]{:S(2)}) copy-start(f32[32,4096]{1,0:T(8,128)} %expand.1) | copy-start | bytes 1572868
  194.5 6.0 %copy-start.3 = (f32[32,4096]{1,0:T(8,128)S(1)}, f32[32,4096]{1,0:T(8,128)}, u32[]{:S(2)}) copy-start(f32[32,4096]{1,0:T(8,128)} %param.44) | copy-start | bytes 1572868
  194.5 6.0 %copy-start.4 = (f32[32,4096]{1,0:T(8,128)S(1)}, f32[32,4096]{1,0:T(8,128)}, u32[]{:S(2)}) copy-start(f32[32,4096]{1,0:T(8,128)} %param.38) | copy-start | bytes 1572868
  194.5 6.0 %copy-start.9 = (f32[32,4096]{1,0:T(8,128)S(1)}, f32[32,4096]{1,0:T(8,128)}, u32[]{:S(2)}) copy-start(f32[32,4096]{1,0:T(8,128)} %get-tuple-element.37) | copy-start | bytes 1572868
  200.5 2.4 %copy-start.5 = (f32[128,1024]{1,0:T(8,128)S(1)}, f32[128,1024]{1,0:T(8,128)}, u32[]{:S(2)}) copy-start(f32[128,1024]{1,0:T(8,128)} %shrink.1) | copy-start | bytes 1572868
  200.5 2.4 %copy-start.6 = (f32[128,1024]{1,0:T(8,128)S(1)}, f32[128,1024]{1,0:T(8,128)}, u32[]{:S(2)}) copy-start(f32[128,1024]{1,0:T(8,128)} %param.45) | copy-start | bytes 1572868
  200.5 2.4 %copy-start.7 = (f32[128,1024]{1,0:T(8,128)S(1)}, f32[128,1024]{1,0:T(8,128)}, u32[]{:S(2)}) copy-start(f32[128,1024]{1,0:T(8,128)} %param.39) | copy-start | bytes 1572868
  200.5 2.4 %copy-start.8 = (f32[128,1024]{1,0:T(8,128)S(1)}, f32[128,1024]{1,0:T(8,128)}, u32[]{:S(2)}) copy-start(f32[128,1024]{1,0:T(8,128)} %get-tuple-element.38) | copy-start | bytes 1572868
  202.8 2.4 %copy-start.16 = (f32[16,512]{1,0:T(8,128)S(1)}, f32[16,512]{1,0:T(8,128)}, u32[]{:S(2)}) copy-start(f32[16,512]{1,0:T(8,128)} %get-tuple-element.39) | copy-start | bytes 98308
  202.8 2.5 %copy-start.19 = (f32[2,32]{1,0:T(2,128)S(1)}, f32[2,32]{1,0:T(2,128)}, u32[]{:S(2)}) copy-start(f32[2,32]{1,0:T(2,128)} %param.34) | copy-start | bytes 772
  202.8 2.5 %copy-start.20 = (f32[2,32]{1,0:T(2,128)S(1)}, f32[2,32]{1,0:T(2,128)}, u32[]{:S(2)}) copy-start(f32[2,32]{1,0:T(2,128)} %param.46) | copy-start | bytes 772
  202.8 2.5 %copy-start.21 = (f32[2,32]{1,0:T(2,128)S(1)}, f32[2,32]{1,0:T(2,128)}, u32[]{:S(2)}) copy-start(f32[2,32]{1,0:T(2,128)} %param.40) | copy-start | bytes 772
  202.8 3.7 %copy-start.18 = (f32[160]{0:T(256)S(1)}, f32[160]{0:T(256)}, u32[]{:S(2)}) copy-start(f32[160]{0:T(256)} %param.35) | copy-start | bytes 1924
  202.8 3.7 %copy-start.22 = (f32[160]{0:T(256)S(1)}, f32[160]{0:T(256)}, u32[]{:S(2)}) copy-start(f32[160]{0:T(256)} %param.47) | copy-start | bytes 1924
  202.8 3.7 %copy-start.23 = (f32[160]{0:T(256)S(1)}, f32[160]{0:T(256)}, u32[]{:S(2)}) copy-start(f32[160]{0:T(256)} %param.41) | copy-start | bytes 1924
  202.9 5.0 %copy-start.1 = (bf16[512,1024]{1,0:T(8,128)(2,1)S(1)}, bf16[512,1024]{1,0:T(8,128)(2,1)}, u32[]{:S(2)}) copy-start(bf16[512,1024]{1,0:T(8,128)(2,1)} %get-tuple-element.98) | copy-start | bytes 3145732
  202.9 5.9 %copy-start = (f32[512,1024]{1,0:T(8,128)S(1)}, f32[512,1024]{1,0:T(8,128)}, u32[]{:S(2)}) copy-start(f32[512,1024]{1,0:T(8,128)} %get-tuple-element.99) | copy-start | bytes 6291460
where the time goes:
time: 210 us
  Pallas kernels  190 us (90%)
  other arithmetic  11.5 us (5%)
  local copies, waits for them, and re-layouts  6.15 us (3%)
  between operations  2.47 us (1%)
    pallas_call x1, Pallas kernels, core(): pl.pallas_call(functools.partial(block_kernel, p), out_shape=shapes, in_s...  190 us
    convert_element_type x6, other arithmetic, adam_update(): return (updated, updated.astype(BF), drift, power)  11.5 us

commit v1 on v0

--- a/solution.py
+++ b/solution.py
@@ -82,11 +82,11 @@
 MESH = pl.DeviceIdType.MESH
 BLOCK = 256
 ATTEND_SHARE = 14
-LATE = 2
+LATE = 1
 AB_START = 1.0
 AB_STEP = 6.0
 C_START = 0.5
-C_STEP = 5.0
+C_STEP = 4.0
 
 
 def turned(a, cosine, sine, back):
@@ -300,14 +300,21 @@
         for way, hop in shares():
             gather_share(k, way, hop, False).wait_send()
 
+    tail_group = C + 3
+
     def scatter_refs(k):
         if k == 0:
-            return wa, sib_a, slot_a, 6 * rq
+            return wa, sib_a, slot_a, 0, 6 * rq
         if k == 1:
-            return wb, sib_b, slot_b, 2 * p.mr
-        if k < C + 2:
-            return wc.at[k - 2], sib_c.at[k - 2], slot_c.at[k - 2], p.c_rows
-        return ws, sib_s, slot_s, 16
+            return wb, sib_b, slot_b, 0, 2 * p.mr
+        if k == C + 2:
+            return ws, sib_s, slot_s, 0, 16
+        j = C - 1 if k == tail_group else k - 2
+        first, count = (0, p.c_rows) if j < C - 1 else (0, 2 * rq)
+        if k == tail_group:
+            first, count = 2 * rq, p.c_rows - 2 * rq
+        cut = pl.ds(first, count)
+        return wc.at[j], sib_c.at[j, :, cut], slot_c.at[j, :, cut], first, count
 
     def swap_copy(ref, src, dst, sem):
         return remote(ref.at[src], ref.at[dst], sw_send.at[sem], sw_recv.at[sem], partner)
@@ -326,6 +333,11 @@
 
     def half_lanes(t, which):
         return pl.ds(pl.multiple_of(t * D + which * W, W), W)
+
+    def shrink_result(j, total):
+        for t in range(p.wb):
+            part = total[t * q : (t + 1) * q]
+            gshr_out[j * q : (j + 1) * q, t * CW : (t + 1) * CW] = part
 
     def scatter_result(k, total):
         if k == 0:
@@ -348,31 +360,32 @@
             keep_exp[j * rq : (j + 1) * rq] = keep
             sw_exp[0, j * rq : (j + 1) * rq] = give.astype(SD)
             exp_back(j).start()
-            for t in range(p.wb):
-                part = total[2 * rq + t * q : 2 * rq + (t + 1) * q]
-                gshr_out[j * q : (j + 1) * q, t * CW : (t + 1) * CW] = part
+            if j < C - 1:
+                shrink_result(j, total[2 * rq :])
+        elif k == tail_group:
+            shrink_result(C - 1, total)
         else:
             sw_small[0] = total
             swap_copy(sw_small, 0, 2, 6).start()
 
     def scatter_sibling(k):
-        whole, sib, _, rows = scatter_refs(k)
-        src = whole.at[:, 1 - core, pl.ds(0, rows)]
+        whole, sib, _, first, rows = scatter_refs(k)
+        src = whole.at[:, 1 - core, pl.ds(first, rows)]
         return remote(src, sib, ss_send.at[k], ss_recv.at[k], sibling)
 
     def slot_of(way, hop):
         return (hop - 1) if way == 0 else half + hop - 1
 
     def scatter_copy(k, way, hop):
-        whole, _, slots, rows = scatter_refs(k)
+        whole, _, slots, first, rows = scatter_refs(k)
         target = around((last_hop(way) + 1 - hop) * (1 - 2 * way))
-        src = whole.at[target, core, pl.ds(0, rows)]
+        src = whole.at[target, core, pl.ds(first, rows)]
         return remote(
             src, slots.at[slot_of(way, hop)], rs_send.at[k, way, hop], rs_recv.at[k, way, hop], ways[way]
         )
 
     def scatter_event(k, hop):
-        whole, sib, slots, rows = scatter_refs(k)
+        whole, sib, slots, first, rows = scatter_refs(k)
         if hop == 0:
             scatter_sibling(k).start()
             return
@@ -381,7 +394,7 @@
         for way in range(2):
             if hop <= last_hop(way):
                 target = around((last_hop(way) + 1 - hop) * (1 - 2 * way))
-                here = whole.at[target, core, pl.ds(0, rows)]
+                here = whole.at[target, core, pl.ds(first, rows)]
                 total = here[...].astype(F32) + sib[target].astype(F32)
                 if hop > 1:
                     scatter_copy(k, way, hop - 1).wait_recv()
@@ -389,7 +402,7 @@
                 here[...] = total.astype(BF)
                 scatter_copy(k, way, hop).start()
         if hop == half + 1:
-            total = whole[chip, core, pl.ds(0, rows)].astype(F32) + sib[chip].astype(F32)
+            total = whole[chip, core, pl.ds(first, rows)].astype(F32) + sib[chip].astype(F32)
             for way in range(2):
                 scatter_copy(k, way, last_hop(way)).wait_recv()
                 total = total + slots[slot_of(way, last_hop(way))].astype(F32)
@@ -424,7 +437,6 @@
     swap_copy(sw_mix, 0, 1, 0).start()
     sw_small[0] = small_own[...]
     swap_copy(sw_small, 0, 1, 1).start()
-    row_copy(0, 0, False).start()
     for load in loads[3:]:
         load.wait()
     mer[0] = jnp.zeros((2 * p.mr, W), BF)
@@ -445,6 +457,7 @@
         wb[chip, core] = mer[0]
 
     swap_copy(sw_mix, 0, 1, 0).wait_recv()
+    row_copy(0, 0, False).start()
     swap_copy(sw_small, 0, 1, 1).wait_recv()
     for t in range(3):
         got = sw_mix[1, t * rq : (t + 1) * rq].astype(F32)
@@ -452,12 +465,6 @@
         wa[chip, core, 2 * t * rq : 2 * (t + 1) * rq] = both_halves
     wa[chip, core, 6 * rq : 6 * rq + 16] = (sw_small[0] + sw_small[1]).astype(BF)
     gather_start(0)
-
-    @pl.when(moves)
-    def _():
-        mer_copy((chip, core)).wait_recv()
-
-    gather_start(1)
     per_lane = 128 // q
 
     def pieces(fetch, width):
@@ -534,10 +541,19 @@
     out[...] = jnp.zeros((p.rows, D), F32)
     for hop in range(1, half + 1):
         gather_event(0, hop)
-        gather_event(1, hop)
+        if hop == 1:
+
+            @pl.when(moves)
+            def _():
+                mer_copy((chip, core)).wait_recv()
+
+            gather_start(1)
+        else:
+            gather_event(1, hop - 1)
         if hop == half - 1:
             chunk_shards()
             gather_start(2)
+    gather_event(1, half)
     for j in range(1, C):
         gather_start(2 + j)
     swap_copy(sw_mix, 0, 1, 0).wait_send()
@@ -645,34 +661,28 @@
         qb, dab = lanes[at_q + t, rows], lanes[at_da + t, rows]
         keys, values = lanes[at_k + t, :width], lanes[at_v + t, :width]
         zero = jnp.zeros_like(qb)
-        mixed = []
-        dquery = []
-        dkey = jnp.zeros((width, 128), F32)
-        dvalue = jnp.zeros((width, 128), F32)
-        for h in range(2):
-            mine = (lane < HEAD) if h == 0 else (lane >= HEAD)
-            qm = jnp.where(mine, qb, zero)
-            dm = jnp.where(mine, dab, zero)
-            scores = dot_right(qm, keys)
-            down = lax.broadcasted_iota(jnp.int32, (BLOCK, BLOCK), 0)
-            over = lax.broadcasted_iota(jnp.int32, (BLOCK, BLOCK), 1)
-            edge = jnp.where(down >= over, scores[:, width - BLOCK :], masked_score)
-            scores = jnp.concatenate([scores[:, : width - BLOCK], edge], axis=1) if i else edge
-            weights = jnp.exp(scores - jnp.max(scores, axis=1, keepdims=True))
-            weights = weights * (1.0 / jnp.sum(weights, axis=1, keepdims=True))
-            rounded = weights.astype(BF)
-            dweights = dot_right(dm, values)
-            delta = jnp.sum(weights * dweights, axis=1, keepdims=True)
-            dscores = (weights * (dweights - delta)).astype(BF)
-            mixed.append(dot(rounded, values))
-            dquery.append(dot(dscores, keys))
-            dvalue = dvalue + dot_left(rounded, dm)
-            dkey = dkey + dot_left(dscores, qm)
         first = lane < HEAD
+        qm = jnp.concatenate([jnp.where(first, qb, zero), jnp.where(first, zero, qb)], axis=0)
+        dm = jnp.concatenate([jnp.where(first, dab, zero), jnp.where(first, zero, dab)], axis=0)
+        scores = dot_right(qm, keys)
+        down = lax.rem(lax.broadcasted_iota(jnp.int32, (2 * BLOCK, BLOCK), 0), BLOCK)
+        over = lax.broadcasted_iota(jnp.int32, (2 * BLOCK, BLOCK), 1)
+        edge = jnp.where(down >= over, scores[:, width - BLOCK :], masked_score)
+        scores = jnp.concatenate([scores[:, : width - BLOCK], edge], axis=1) if i else edge
+        weights = jnp.exp(scores - jnp.max(scores, axis=1, keepdims=True))
+        weights = weights * (1.0 / jnp.sum(weights, axis=1, keepdims=True))
+        rounded = weights.astype(BF)
+        dweights = dot_right(dm, values)
+        delta = jnp.sum(weights * dweights, axis=1, keepdims=True)
+        dscores = (weights * (dweights - delta)).astype(BF)
+        mixed = dot(rounded, values)
+        dquery = dot(dscores, keys)
+        dvalue = dot_left(rounded, dm)
+        dkey = dot_left(dscores, qm)
         position = lax.broadcasted_iota(jnp.int32, (BLOCK, 128), 0) + i * BLOCK
-        whole = jnp.where(first, mixed[0], mixed[1])
+        whole = jnp.where(first, mixed[:BLOCK], mixed[BLOCK:])
         lanes[at_att + t, rows] = jnp.where(position < length[0], whole, 0.0).astype(BF)
-        dq = jnp.where(first, dquery[0], dquery[1]) * HEAD**-0.5
+        dq = jnp.where(first, dquery[:BLOCK], dquery[BLOCK:]) * HEAD**-0.5
         lanes[at_q + t, rows] = turned(dq, cos_ref[rows], sin_ref[rows], True).astype(BF)
         out[:width, head_lanes(t, 0)] += dkey
         out[:width, head_lanes(t, 1)] += dvalue
@@ -791,6 +801,7 @@
         for j in range(C):
             begin = grad_at[j] + 2 + C_START
             timed.append((begin + (hop - 1) * C_STEP * pace, 2 + j, hop))
+        timed.append((begin + 0.5 + (hop - 1) * C_STEP * pace, tail_group, hop))
     timed.sort()
     slots = [[e[1:] for e in timed if t <= e[0] < t + 1] for t in range(total_slots)]
     leftover = [e[1:] for e in timed if e[0] >= total_slots]
@@ -865,6 +876,8 @@
             return carry
 
         lax.fori_loop(0, D // BLOCK, expand_grads, 0)
+        if j == C - 1:
+            scatter_event(2 + j, 0)
         run_slot(grad_at[j])
         per = BLOCK // (2 * q)
 
@@ -877,7 +890,7 @@
             return carry
 
         lax.fori_loop(0, CW // BLOCK, shrink_grads, 0)
-        scatter_event(2 + j, 0)
+        scatter_event(2 + j if j < C - 1 else tail_group, 0)
         run_slot(grad_at[j] + 1)
 
     for kind, j in order:
@@ -944,7 +957,7 @@
         if k == C + 1 and hop == half + 1:
             finish_all()
         scatter_event(k, hop)
-        if k == C + 1:
+        if k == tail_group:
             if hop == 1:
                 small_gradients()
             else:
@@ -1023,10 +1036,10 @@
         dma((C + 2, 2, half + 1)),
         dma((C + 2,)),
         dma((C + 2,)),
-        dma((C + 3, 2, half + 1)),
-        dma((C + 3, 2, half + 1)),
-        dma((C + 3,)),
-        dma((C + 3,)),
+        dma((C + 4, 2, half + 1)),
+        dma((C + 4, 2, half + 1)),
+        dma((C + 4,)),
+        dma((C + 4,)),
         dma((6,)),
         dma((6,)),
         dma((7 + p.FF // D,)),

time: 210 us -> 203 us (0.967)
  Pallas kernels: 190 us -> 183 us
    pallas_call x1, Pallas kernels: 190 us -> 183 us  [core(): pl.pallas_call(functools.partial(block_kernel, p), out_shape=shapes, in_s...]
where the time goes in v1:
time: 203 us
  Pallas kernels  183 us (90%)
  other arithmetic  11.5 us (6%)
  local copies, waits for them, and re-layouts  6.15 us (3%)
  between operations  2.47 us (1%)
    pallas_call x1, Pallas kernels, core(): pl.pallas_call(functools.partial(block_kernel, p), out_shape=shapes, in_s...  183 us
    convert_element_type x6, other arithmetic, adam_update(): return (updated, updated.astype(BF), drift, power)  11.5 us

profile of v1, /device:TPU:0, one launch (start us, length us, event | category | flops | bytes accessed | tf_op | source)
XLA Modules:
  0.0 202.8 jit_solution(2060406461003056576)
XLA Ops:
  0.7 0.8 bitcast_dynamic-update-slice_fusion.1
  1.5 0.8 bitcast_dynamic-update-slice_fusion
  2.3 0.9 dynamic_update_slice.11
  3.1 0.6 reshape.67.small_own
  4.4 0.0 copy-start.17
  4.4 0.0 copy-start.10
  4.4 0.0 copy-start.11
  4.4 182.7 %shard_map.440 = (bf16[512,1024]{1,0:T(8,128)(2,1)}, f32[512,1024]{1,0:T(8,128)}, f32[32,3072]{1,0:T(8,128)}, f32[32,1024]{1,0:T(8,128)}, f32[32,4096]{1,0:T(8,1...) custom-call(bf16[512,1024]{1,0:T(8,128)(2,1)} %stream.1, bf16[512,1024]{1,0:T(8,128)(2,1)} %cotangent.1, f32[32,3072]{1,0:T(8,128)} %mixing.1, ...), custom_call_target="tpu_custom_call" | custom-call | flops 45097156608 | bytes 8388608 | tf_op jit(solution)/shard_map/pallas_call | solution.py:1066
  187.2 0.0 copy-start.12
  187.2 0.0 copy-start.13
  187.2 0.0 copy-start.14
  187.2 0.0 copy-start.15
  187.2 0.0 copy-start.2
  187.2 0.0 copy-start.3
  187.2 0.0 copy-start.4
  187.2 0.0 copy-start.9
  188.1 0.0 copy-done.17
  188.1 0.6 fusion.18
  188.8 0.0 copy-done.10
  188.8 0.0 copy-done.11
  188.8 3.0 %fusion.16 = (bf16[32,3072]{1,0:T(8,128)(2,1)}, f32[32,3072]{1,0:T(8,128)}, f32[32,3072]{1,0:T(8,128)}, f32[32,3072]{1,0:T(8,128)}) fusion(f32[32,3072]{1,0:T(8,128)S(1)} %copy-done.10, f32[]{:T(128)} %bitcast.4, f32[]{:T(128)} %bitcast.3, f32[]{:T(128)} %bitcast.2, f32[32,3072]{1,0:T(8,128)} %get-tuple-element.35, f32[32,3072]{1,0:T(8,128)S(1)} %copy-done.11, ...), kind=kLoop, calls=%fused_computation.34 | loop fusion | flops 1572864 | bytes 2949132 | tf_op jit(solution)/shard_map/convert_element_type | solution.py:56
  191.8 0.0 copy-done.12
  191.8 0.0 copy-done.13
  191.8 0.0 copy-done.14
  191.8 0.0 copy-done.15
  191.8 1.5 fusion.14
  193.2 0.0 copy-start.5
  193.2 0.0 copy-start.6
  193.2 0.0 copy-start.7
  193.2 0.0 copy-start.8
  193.2 0.0 copy-done.2
  193.3 0.0 copy-done.3
  193.3 0.0 copy-done.4
  193.3 0.0 copy-done.9
  193.3 2.3 %fusion.12 = (bf16[32,4096]{1,0:T(8,128)(2,1)}, f32[32,4096]{1,0:T(8,128)}, f32[32,4096]{1,0:T(8,128)}, f32[32,4096]{1,0:T(8,128)}) fusion(f32[32,4096]{1,0:T(8,128)S(1)} %copy-done.2, f32[]{:T(128)} %bitcast.4, f32[]{:T(128)} %bitcast.3, f32[]{:T(128)} %bitcast.6, f32[32,4096]{1,0:T(8,128)S(1)} %copy-done.9, f32[32,4096]{1,0:T(8,128)S(1)} %copy-done.3, ...), kind=kLoop, calls=%fused_computation.32 | loop fusion | flops 2097152 | bytes 3932172 | tf_op jit(solution)/shard_map/convert_element_type | solution.py:56
  195.5 0.0 copy-start.16
  195.5 0.0 copy-start.19
  195.5 0.0 copy-start.20
  195.5 0.0 copy-start.21
  195.6 0.0 copy-start.18
  195.6 0.0 copy-start.22
  195.6 0.0 copy-start.23
  195.6 0.0 copy-start.1
  195.6 0.0 copy-done.5
  195.6 0.0 copy-done.6
  195.6 0.0 copy-done.7
  195.6 0.0 copy-done.8
  195.6 0.0 copy-start
  195.7 2.3 %fusion.10 = (bf16[128,1024]{1,0:T(8,128)(2,1)}, f32[128,1024]{1,0:T(8,128)}, f32[128,1024]{1,0:T(8,128)}, f32[128,1024]{1,0:T(8,128)}) fusion(f32[128,1024]{1,0:T(8,128)S(1)} %copy-done.5, f32[]{:T(128)} %bitcast.4, f32[]{:T(128)} %bitcast.3, f32[]{:T(128)} %bitcast.7, f32[128,1024]{1,0:T(8,128)S(1)} %copy-done.8, f32[128,1024]{1,0:T(8,128)S(1)} %copy-done.6, ...), kind=kLoop, calls=%fused_computation.31 | loop fusion | flops 2097152 | bytes 3932172 | tf_op jit(solution)/shard_map/convert_element_type | solution.py:56
  197.9 0.0 copy-done.16
  198.0 0.1 dynamic-slice_bitcast_fusion.1
  198.0 0.0 copy-done.19
  198.0 0.0 copy-done.20
  198.0 0.0 copy-done.21
  198.1 1.2 fusion.8
  199.3 0.0 copy-done.18
  199.3 0.0 copy-done.22
  199.3 0.0 copy-done.23
  199.3 1.2 fusion.6
  200.5 0.0 copy-done.1
  200.5 1.0 copy.59
  201.5 0.0 copy-done
  201.5 1.3 copy.60
  (2 shorter events, 0.0 us)
Async XLA Ops:
  4.4 183.8 %copy-start.17 = (f32[6]{0:T(128)S(1)}, f32[6]{0:T(128)}, u32[]{:S(2)}) copy-start(f32[6]{0:T(128)} %param.29) | copy-start | bytes 76
  4.4 184.4 %copy-start.10 = (f32[32,3072]{1,0:T(8,128)S(1)}, f32[32,3072]{1,0:T(8,128)}, u32[]{:S(2)}) copy-start(f32[32,3072]{1,0:T(8,128)} %mixing.1) | copy-start | bytes 1179652
  4.4 184.4 %copy-start.11 = (f32[32,3072]{1,0:T(8,128)S(1)}, f32[32,3072]{1,0:T(8,128)}, u32[]{:S(2)}) copy-start(f32[32,3072]{1,0:T(8,128)} %param.42) | copy-start | bytes 1179652
  187.2 4.6 %copy-start.12 = (f32[32,1024]{1,0:T(8,128)S(1)}, f32[32,1024]{1,0:T(8,128)}, u32[]{:S(2)}) copy-start(f32[32,1024]{1,0:T(8,128)} %merging.1) | copy-start | bytes 393220
  187.2 4.6 %copy-start.13 = (f32[32,1024]{1,0:T(8,128)S(1)}, f32[32,1024]{1,0:T(8,128)}, u32[]{:S(2)}) copy-start(f32[32,1024]{1,0:T(8,128)} %param.43) | copy-start | bytes 393220
  187.2 4.6 %copy-start.14 = (f32[32,1024]{1,0:T(8,128)S(1)}, f32[32,1024]{1,0:T(8,128)}, u32[]{:S(2)}) copy-start(f32[32,1024]{1,0:T(8,128)} %param.37) | copy-start | bytes 393220
  187.2 4.6 %copy-start.15 = (f32[32,1024]{1,0:T(8,128)S(1)}, f32[32,1024]{1,0:T(8,128)}, u32[]{:S(2)}) copy-start(f32[32,1024]{1,0:T(8,128)} %get-tuple-element.36) | copy-start | bytes 393220
  187.2 6.0 %copy-start.2 = (f32[32,4096]{1,0:T(8,128)S(1)}, f32[32,4096]{1,0:T(8,128)}, u32[]{:S(2)}) copy-start(f32[32,4096]{1,0:T(8,128)} %expand.1) | copy-start | bytes 1572868
  187.2 6.0 %copy-start.3 = (f32[32,4096]{1,0:T(8,128)S(1)}, f32[32,4096]{1,0:T(8,128)}, u32[]{:S(2)}) copy-start(f32[32,4096]{1,0:T(8,128)} %param.44) | copy-start | bytes 1572868
  187.2 6.0 %copy-start.4 = (f32[32,4096]{1,0:T(8,128)S(1)}, f32[32,4096]{1,0:T(8,128)}, u32[]{:S(2)}) copy-start(f32[32,4096]{1,0:T(8,128)} %param.38) | copy-start | bytes 1572868
  187.2 6.0 %copy-start.9 = (f32[32,4096]{1,0:T(8,128)S(1)}, f32[32,4096]{1,0:T(8,128)}, u32[]{:S(2)}) copy-start(f32[32,4096]{1,0:T(8,128)} %get-tuple-element.37) | copy-start | bytes 1572868
  193.2 2.4 %copy-start.5 = (f32[128,1024]{1,0:T(8,128)S(1)}, f32[128,1024]{1,0:T(8,128)}, u32[]{:S(2)}) copy-start(f32[128,1024]{1,0:T(8,128)} %shrink.1) | copy-start | bytes 1572868
  193.2 2.4 %copy-start.6 = (f32[128,1024]{1,0:T(8,128)S(1)}, f32[128,1024]{1,0:T(8,128)}, u32[]{:S(2)}) copy-start(f32[128,1024]{1,0:T(8,128)} %param.45) | copy-start | bytes 1572868
  193.2 2.4 %copy-start.7 = (f32[128,1024]{1,0:T(8,128)S(1)}, f32[128,1024]{1,0:T(8,128)}, u32[]{:S(2)}) copy-start(f32[128,1024]{1,0:T(8,128)} %param.39) | copy-start | bytes 1572868
  193.2 2.4 %copy-start.8 = (f32[128,1024]{1,0:T(8,128)S(1)}, f32[128,1024]{1,0:T(8,128)}, u32[]{:S(2)}) copy-start(f32[128,1024]{1,0:T(8,128)} %get-tuple-element.38) | copy-start | bytes 1572868
  195.5 2.4 %copy-start.16 = (f32[16,512]{1,0:T(8,128)S(1)}, f32[16,512]{1,0:T(8,128)}, u32[]{:S(2)}) copy-start(f32[16,512]{1,0:T(8,128)} %get-tuple-element.39) | copy-start | bytes 98308
  195.5 2.5 %copy-start.19 = (f32[2,32]{1,0:T(2,128)S(1)}, f32[2,32]{1,0:T(2,128)}, u32[]{:S(2)}) copy-start(f32[2,32]{1,0:T(2,128)} %param.34) | copy-start | bytes 772
  195.5 2.5 %copy-start.20 = (f32[2,32]{1,0:T(2,128)S(1)}, f32[2,32]{1,0:T(2,128)}, u32[]{:S(2)}) copy-start(f32[2,32]{1,0:T(2,128)} %param.46) | copy-start | bytes 772
  195.5 2.5 %copy-start.21 = (f32[2,32]{1,0:T(2,128)S(1)}, f32[2,32]{1,0:T(2,128)}, u32[]{:S(2)}) copy-start(f32[2,32]{1,0:T(2,128)} %param.40) | copy-start | bytes 772
  195.6 3.7 %copy-start.18 = (f32[160]{0:T(256)S(1)}, f32[160]{0:T(256)}, u32[]{:S(2)}) copy-start(f32[160]{0:T(256)} %param.35) | copy-start | bytes 1924
  195.6 3.7 %copy-start.22 = (f32[160]{0:T(256)S(1)}, f32[160]{0:T(256)}, u32[]{:S(2)}) copy-start(f32[160]{0:T(256)} %param.47) | copy-start | bytes 1924
  195.6 3.7 %copy-start.23 = (f32[160]{0:T(256)S(1)}, f32[160]{0:T(256)}, u32[]{:S(2)}) copy-start(f32[160]{0:T(256)} %param.41) | copy-start | bytes 1924
  195.6 5.0 %copy-start.1 = (bf16[512,1024]{1,0:T(8,128)(2,1)S(1)}, bf16[512,1024]{1,0:T(8,128)(2,1)}, u32[]{:S(2)}) copy-start(bf16[512,1024]{1,0:T(8,128)(2,1)} %get-tuple-element.98) | copy-start | bytes 3145732
  195.6 5.9 %copy-start = (f32[512,1024]{1,0:T(8,128)S(1)}, f32[512,1024]{1,0:T(8,128)}, u32[]{:S(2)}) copy-start(f32[512,1024]{1,0:T(8,128)} %get-tuple-element.99) | copy-start | bytes 6291460
